TPU v7x, 256 devices: a whole 4x4x8 slice. The times are simulated.
256 devices in a mesh: blk: 32 (over z, x_lo, core), cols: 8 (over y, x_hi).
Axes of the slice: x: 4 (x_hi: 2, x_lo: 2; x = x_hi * 2 + x_lo), y: 4, z: 8, core: 2. Of those that a mesh axis runs over, the one named last changes fastest.
Arguments:
- queries: bfloat16 [4096, 768], P('blk'), may hold values from -6 to 6
- label_ids: int32 [4096, 8], P('blk'), may hold values from -1 to 131071, as said below
- weights: float32 [131072, 768], P(('blk', 'cols')), may hold values from -0.21875 to 0.21875
- momentum: float32 [131072, 768], P(('blk', 'cols')), may hold values from -12 to 12
Outputs:
- new_weights: float32 [131072, 768], P(('blk', 'cols'))
- new_momentum: float32 [131072, 768], P(('blk', 'cols'))
- query_grad: float32 [4096, 768], P('blk')
Inputs may be any that keep to these rules, and one draw needn't show every extreme that they name: `label_ids`: each query lists 1 to 8 label ids in its first entries and -1 in the rest; ids may repeat within a list; some query lists 8 ids and some lists one.
All inputs are finite; a program needn't handle non-finite values.
Results may differ from a plain program's by a relative error of at most 0.0027.
Values may be sent and summed in bfloat16 or wider, within the bound.
A program may use at most 128 MiB of HBM per device.

v0:
```python
import jax
import jax.numpy as jnp
from jax import lax
from jax.sharding import PartitionSpec as P

loss_scale = 1.0 / 16.0
keep_rate = 0.9
step_rate = 0.005


def body(queries, label_ids, weights, momentum):
    lab_dev = weights.shape[0]
    offset = (lax.axis_index("blk") * lax.axis_size("cols") + lax.axis_index("cols")) * lab_dev
    w_half = weights.astype(jnp.bfloat16)
    lab_iota = lax.broadcasted_iota(jnp.int32, (1, 1, lab_dev), 2)
    rows = lax.all_gather(queries, "blk", axis=0, tiled=True)
    ids = lax.all_gather(label_ids, "blk", axis=0, tiled=True)
    scores = lax.dot_general(
        rows, w_half, (((1,), (1,)), ((), ())), preferred_element_type=jnp.float32
    )
    local = ids - offset
    target = jnp.any(local[:, :, None] == lab_iota, axis=1).astype(jnp.float32)
    grad = ((jax.nn.sigmoid(scores) - target) * loss_scale).astype(jnp.bfloat16)
    w_grad = lax.dot_general(
        grad, rows, (((0,), (0,)), ((), ())), preferred_element_type=jnp.float32
    )
    grads, w_grad = (grad, w_grad)
    summed = lax.psum_scatter(
        jnp.dot(grads, w_half, preferred_element_type=jnp.float32),
        "blk",
        scatter_dimension=0,
        tiled=True,
    )
    query_grad = lax.psum(summed, "cols")
    new_momentum = keep_rate * momentum + w_grad
    new_weights = weights - step_rate * new_momentum
    return (new_weights, new_momentum, query_grad)


def solution(mesh):
    return jax.shard_map(
        body,
        mesh=mesh,
        in_specs=(
            P("blk", None),
            P("blk", None),
            P(("blk", "cols"), None),
            P(("blk", "cols"), None),
        ),
        out_specs=(P(("blk", "cols"), None), P(("blk", "cols"), None), P("blk", None)),
        check_vma=False,
    )
```

profile of v0, /device:TPU:1, one launch (start us, length us, event | category | flops | bytes accessed | tf_op | source)
XLA Modules:
  0.0 344.0 jit_solution(12885010236975235153)
XLA Ops:
  7.2 0.0 all-gather.2.cloned.1.call-start
  7.2 0.7 all-gather.2.cloned.1.call-update
  7.9 0.0 reduce-scatter.2.cloned.1.call-start
  8.0 39.4 %all_gather.7 = s32[4096,8]{0,1:T(8,128)S(1)} all-gather(s32[128,8]{0,1:T(8,128)} %param.5), channel_id=1, replica_groups=mesh['blk'=32,'cols'=8] {'blk'}, dimensions={0}, use_global_device_ids=true | all-gather | bytes 135168 | tf_op jit(solution)/shard_map/all_gather | solution.py:17
  47.4 0.6 copy.8
  48.0 27.6 %fusion = pred[4096,512]{1,0:T(8,128)(4,1)} fusion(s32[4096,8]{1,0:T(8,128)S(1)} %copy.8), kind=kLoop, calls=%fused_computation.1 | loop fusion | flops 31457280 | bytes 2228224 | tf_op jit(solution)/shard_map/reduce_or | solution.py:22
  75.6 0.0 copy-start.1
  75.6 8.8 %all-gather.2.cloned.1.call-done = bf16[4096,768]{1,0:T(8,128)(2,1)} async-done(((bf16[128,768]{1,0:T(8,128)(2,1)}), bf16[4096,768]{1,0:T(8,128)(2,1)}) %all-gather.2.cloned.1.call-update) | async-done | bytes 6291472 | tf_op jit(solution)/shard_map/all_gather | solution.py:16
  84.4 8.9 %multiply_convert_fusion = bf16[4096,512]{1,0:T(8,128)(2,1)S(1)} fusion(pred[4096,512]{1,0:T(8,128)(4,1)} %fusion, bf16[4096,768]{1,0:T(8,128)(2,1)} %all-gather.2.cloned.1.call-done, f32[512,768]{1,0:T(8,128)} %param.6), kind=kOutput, calls=%fused_computation.2 | convolution fusion | flops 3236298752 | bytes 14155776 | tf_op jit(solution)/shard_map/dot_general | solution.py:18
  93.3 0.0 copy-start
  93.3 2.0 copy-done
  95.3 0.0 copy-done.1
  95.3 6.4 %fusion.1 = f32[4096,768]{1,0:T(8,128)} fusion(bf16[4096,512]{1,0:T(8,128)(2,1)S(1)} %multiply_convert_fusion, f32[512,768]{1,0:T(8,128)S(1)} %copy-done.1), kind=kOutput, calls=%fused_computation.5 | convolution fusion | flops 3221618688 | bytes 18350080 | tf_op jit(solution)/shard_map/dot_general | solution.py:29
  101.7 0.0 copy-start.2
  101.8 0.0 reduce-scatter.2.cloned.1.call-update
  101.8 0.2 all-reduce.2.cloned.1.call-start
  102.0 149.0 %reduce-scatter.2.cloned.1.call-done = f32[128,768]{1,0:T(8,128)} async-done(((f32[4096,768]{1,0:T(8,128)}), f32[128,768]{1,0:T(8,128)}) %reduce-scatter.2.cloned.1.call-update) | async-done | bytes 393232 | tf_op jit(solution)/shard_map/reduce_scatter | solution.py:28
  251.0 0.0 all-reduce.2.cloned.1.call-update
  251.0 0.0 copy-done.2
  251.0 9.3 %multiply_subtract_fusion = (f32[512,768]{1,0:T(8,128)}, f32[512,768]{1,0:T(8,128)}) fusion(f32[512,768]{1,0:T(8,128)S(1)} %copy-done.1, bf16[4096,512]{1,0:T(8,128)(2,1)} %copy-done, bf16[4096,768]{1,0:T(8,128)(2,1)} %all-gather.2.cloned.1.call-done, f32[512,768]{1,0:T(8,128)S(1)} %copy-done.2), kind=kOutput, calls=%fused_computation.3 | convolution fusion | flops 3222798336 | bytes 16777216 | tf_op jit(solution)/shard_map/dot_general | solution.py:24
  260.3 75.3 %all-reduce.2.cloned.1.call-done = f32[128,768]{1,0:T(8,128)} async-done(((f32[128,768]{1,0:T(8,128)}), f32[128,768]{1,0:T(8,128)}) %all-reduce.2.cloned.1.call-update) | async-done | bytes 393232 | tf_op jit(solution)/shard_map/psum | solution.py:34
  335.7 1.8 copy.10
  (1 shorter events, 0.0 us)
Async XLA Ops:
  7.2 77.2 %all-gather.2.cloned.1.call-start = ((), (), s32[]{:S(2)}) async-start(), calls=%async_computation.1 | async-start | bytes 6488064 | tf_op jit(solution)/shard_map/all_gather | solution.py:16
  7.9 243.1 %reduce-scatter.2.cloned.1.call-start = ((), (), s32[]{:S(2)}) async-start(), calls=%async_computation.2 | async-start | bytes 12976128 | tf_op jit(solution)/shard_map/reduce_scatter | solution.py:28
  75.6 19.7 %copy-start.1 = (f32[512,768]{1,0:T(8,128)S(1)}, f32[512,768]{1,0:T(8,128)}, u32[]{:S(2)}) copy-start(f32[512,768]{1,0:T(8,128)} %param.6) | copy-start | bytes 4718596
  93.3 2.0 copy-start
  101.7 149.3 %copy-start.2 = (f32[512,768]{1,0:T(8,128)S(1)}, f32[512,768]{1,0:T(8,128)}, u32[]{:S(2)}) copy-start(f32[512,768]{1,0:T(8,128)} %param.7) | copy-start | bytes 4718596
  101.8 233.9 %all-reduce.2.cloned.1.call-start = ((), (), s32[]{:S(2)}) async-start(), calls=%async_computation.3 | async-start | bytes 786432 | tf_op jit(solution)/shard_map/psum | solution.py:34
Sparse Core Ops, SparseCore 0:
  9.9 74.4 all-gather.1
  101.9 149.0 reduce-scatter.1
  253.6 82.0 all-reduce.1
where the time goes:
time: 348 us; the launch traced here: 344 us
  waiting for transfers between devices  234 us (67%)
  blocking collectives  39.4 us (11%)
  other arithmetic  27.6 us (8%)
  matrix products  24.6 us (7%)
  between operations  13.8 us (4%)
  local copies, waits for them, and re-layouts  4.39 us (1%)
    reduce_scatter x1, waiting for transfers between devices, body(): lax.psum_scatter(jnp.dot(grads, w_half, preferred_element_type=jnp.float3...  149 us
    psum x1, waiting for transfers between devices, body(): query_grad = lax.psum(summed, 'cols')  75.3 us
    all_gather x1, blocking collectives, body(): ids = lax.all_gather(label_ids, 'blk', axis=0, tiled=True)  39.4 us
    reduce_or x1, other arithmetic, body(): target = jnp.any(local[:, :, None] == lab_iota, axis=1).astype(jnp.float32)  27.6 us
    dot_general x1, matrix products, body(): lax.dot_general(grad, rows, (((0,), (0,)), ((), ())), preferred_element_t...  9.3 us
    dot_general x1, matrix products, body(): lax.dot_general(rows, w_half, (((1,), (1,)), ((), ())), preferred_element...  8.92 us
    all_gather x1, waiting for transfers between devices, body(): rows = lax.all_gather(queries, 'blk', axis=0, tiled=True)  8.77 us
  transfers between devices with their start and end apart: 3, of which 3 were waited for; matrix products, arithmetic and copies ran while one was open for 11% of the time, Pallas kernels for 0%

commit v1 on v0

v1 whole, which is shorter than its diff:
```python
import functools

import jax
import jax.numpy as jnp
from jax import lax
from jax.experimental import pallas as pl
from jax.experimental.pallas import tpu as pltpu
from jax.sharding import PartitionSpec as P

MESH = pl.DeviceIdType.MESH
F32, BF16 = jnp.float32, jnp.bfloat16
NT = (((1,), (1,)), ((), ()))
TN = (((0,), (0,)), ((), ()))
NN = (((1,), (0,)), ((), ()))

loss_scale = 1.0 / 16.0
keep_rate = 0.9
step_rate = 0.005

D = 768
LAB = 512
QB = 128
ZN, YN, XN = 8, 4, 4
LIST = 8
SUB = 4
PIECE = LAB // 2 // SUB
PLACE = {1: 0, 7: 1, 2: 2, 6: 3, 3: 4, 5: 5, 4: 6, 0: 7}
QUARTER = QB // 4


def dot(a, b, dims):
    return lax.dot_general(a, b, dims, preferred_element_type=F32)


def device(z, y, x, core):
    return (z * 4 + (x % 2) * 2 + core, y * 2 + x // 2)


def copy_names():
    names = []
    for way in "+-":
        for step in range(1, 5):
            for quarter in range(2):
                if step < 4 or quarter == (0 if way == "+" else 1):
                    names.append(("zg", way, step, quarter))
            if step < 4 or way == "+":
                names.append(("id", way, step))
    names += [("yg", r, k) for r in range(1, 8) for k in range(2)]
    names += [("cw",)]
    names += [(kind, way, i) for kind in ("xw", "fw", "gc", "gx") for way in "+-" for i in range(SUB)]
    names += [("go", i) for i in range(2)]
    names += [("yr", r, k) for r in range(8) for k in range(2)]
    for way in "+-":
        for step in range(1, 5):
            for quarter in range(2):
                if step > 1 or quarter == (0 if way == "+" else 1):
                    names.append(("zr", way, step, quarter))
    names += [("rs", k) for k in range(1, 4)]
    names += [("ag", k) for k in range(1, 8)]
    return names


NAMES = {name: i for i, name in enumerate(copy_names())}


def kernel(
    q_in, ids_in, w_in, wg_out, qg_out,
    Q, IDS, M, WF, W, WG, QG, YS, YR, ZS, ZR, GOS, GOR, GCS, GCR, GXS, GXR, RS, RR, OUT, local_sem, send_sem, recv_sem,
):
    blk, cols = lax.axis_index("blk"), lax.axis_index("cols")
    z, xl, core = blk // 4, (blk // 2) % 2, blk % 2
    y, xh = cols // 2, cols % 2
    x = xh * 2 + xl
    p = y % 2

    z_of = {"+": device((z + 1) % ZN, y, x, core), "-": device((z + ZN - 1) % ZN, y, x, core)}
    y_of = {"+": device(z, (y + 1) % YN, x, core), "-": device(z, (y + YN - 1) % YN, x, core)}
    x_of = {"+": device(z, y, (x + 1) % XN, core), "-": device(z, y, (x + XN - 1) % XN, core)}
    partner = device(z, y, x, 1 - core)
    far_x = (x + 2) % XN
    same = {k: device(z, (y + k // 2) % YN, far_x if k % 2 else x, core) for k in range(1, 8)}

    cq = pltpu.make_async_copy(q_in, Q.at[pl.ds(PLACE[0] * QB, QB)], local_sem.at[0])
    cq.start()
    cw = pltpu.make_async_copy(w_in, WF, local_sem.at[1])
    cw.start()

    barrier = pltpu.get_barrier_semaphore()
    greeted = [partner] + [t[w] for t in (z_of, x_of) for w in "+-"] + list(same.values())
    for d in greeted:
        pl.semaphore_signal(barrier, inc=1, device_id=d, device_id_type=MESH)

    ids = ids_in[...]
    wide = jnp.concatenate([ids, jnp.zeros((QB, 128 - LIST), jnp.int32)], axis=1)
    IDS[0] = jnp.transpose(wide)[:LIST]

    cps = {}

    def start(name, src, dst, dev):
        cp = pltpu.make_async_remote_copy(
            src_ref=src, dst_ref=dst, send_sem=send_sem.at[NAMES[name]], recv_sem=recv_sem.at[NAMES[name]],
            device_id=dev, device_id_type=MESH,
        )
        cp.start()
        cps[name] = cp

    def arrived(*names):
        for name in names:
            cps[name].wait_recv()

    def rows(slot, half, quarter):
        return pl.ds(pl.multiple_of(PLACE[slot] * QB + half * (QB // 2) + quarter * QUARTER, QUARTER), QUARTER)

    def gather_z(way, step, quarter):
        src, dst = ((9 - step) % 8, 8 - step) if way == "+" else (step - 1, step)
        start(("zg", way, step, quarter), Q.at[rows(src, p, quarter)], Q.at[rows(dst, p, quarter)], z_of[way])

    def gather_ids(way, step):
        src, dst = ((9 - step) % 8, 8 - step) if way == "+" else (step - 1, step)
        start(("id", way, step), IDS.at[src], IDS.at[dst], z_of[way])

    def gather_y(slot, quarter):
        here = Q.at[rows(slot, p, quarter)]
        start(("yg", slot, quarter), here, here, y_of["+-"[quarter]])

    def step_gather(step):
        for quarter in range(2):
            for way in "+-":
                if ("zg", way, step, quarter) not in NAMES:
                    continue
                arrived(("zg", way, step, quarter))
                if ("zg", way, step + 1, quarter) in NAMES:
                    gather_z(way, step + 1, quarter)
                gather_y(8 - step if way == "+" else step, quarter)
        for way in "+-":
            if ("id", way, step) in NAMES:
                arrived(("id", way, step))
                if ("id", way, step + 1) in NAMES:
                    gather_ids(way, step + 1)

    def forward_weights(i):
        for way, base in (("+", 2 * LAB), ("-", 3 * LAB)):
            arrived(("xw", way, i))
            start(("fw", way, i), W.at[pl.ds(base + i * PIECE, PIECE)],
                  W.at[pl.ds(base + LAB // 2 + i * PIECE, PIECE)], partner)

    def first(z, y, x, core):
        b, c = device(z, y, x, core)
        return (b * 8 + c) * LAB

    left, right = (x + XN - 1) % XN, (x + 1) % XN
    half = LAB // 2
    pieces = [
        (0, LAB, first(z, y, x, core)),
        (LAB, LAB, first(z, y, x, 1 - core)),
        (2 * LAB, half, first(z, y, left, core) + half),
        (2 * LAB + half, half, first(z, y, left, 1 - core) + half),
        (3 * LAB, half, first(z, y, right, core)),
        (3 * LAB + half, half, first(z, y, right, 1 - core)),
    ]

    def build_mask(slot):
        ids = IDS[slot]
        row = jnp.full(ids.shape, -1, jnp.int32)
        for base, count, label in pieces:
            local = ids - label
            row = jnp.where((local >= 0) & (local < count), local + base, row)
        low = jnp.where(row >= 0, row % 128, -1)
        bit = jnp.left_shift(1, jnp.maximum(row, 0) // 128)
        sub = lax.broadcasted_iota(jnp.int32, (128, QB), 0)
        m = jnp.zeros((128, QB), jnp.int32)
        for j in range(LIST):
            m = m | jnp.where(low[j:j + 1] == sub, bit[j:j + 1], 0)
        M[PLACE[slot] * QB:(PLACE[slot] + 1) * QB] = jnp.transpose(m)

    seen = set()

    def work(slot, part):
        at = PLACE[slot] * QB
        here, there = slice(at, at + 2 * QB), slice(part * 2 * LAB, (part + 1) * 2 * LAB)
        q, w, m = Q[here], W[there], M[here]
        scores = dot(q, w, NT)
        out = []
        for b in range(2 * LAB // 128):
            target = ((m >> (part * 2 * LAB // 128 + b)) & 1).astype(F32)
            out.append(((jax.nn.sigmoid(scores[:, b * 128:(b + 1) * 128]) - target) * loss_scale).astype(BF16))
        grad = jnp.concatenate(out, axis=1)
        a = dot(grad, w, NN)
        if part == 0:
            QG[here] = a
        else:
            QG[here] += a
        g = dot(grad, q, TN)
        if part not in seen:
            WG[there] = g
        else:
            WG[there] += g
        seen.add(part)

    def reduce_y(slot):
        for k in range(2):
            YS[slot, k] = QG[rows(slot, 1 - p, k)].astype(BF16)
            start(("yr", slot, k), YS.at[slot, k], YR.at[slot, k], y_of["-+"[k]])

    def total(slot, quarter):
        arrived(("yr", slot, quarter))
        t = QG[rows(slot, p, quarter)] + YR[slot, quarter].astype(F32)
        for i, way in enumerate("+-"):
            step = 4 - slot if way == "+" else (slot - 4 if slot else 4)
            if ("zr", way, step, quarter) in NAMES and (slot == 0 or (slot < 4) == (way == "+")):
                arrived(("zr", way, step, quarter))
                t = t + ZR[i, step - 1, quarter].astype(F32)
        return t

    def reduce_z(step):
        for quarter in range(2):
            for i, way in enumerate("+-"):
                if ("zr", way, step, quarter) not in NAMES:
                    continue
                slot = 5 - step if way == "+" else 3 + step
                ZS[i, step - 1, quarter] = total(slot, quarter).astype(BF16)
                start(("zr", way, step, quarter), ZS.at[i, step - 1, quarter], ZR.at[i, step - 1, quarter], z_of[way])

    cq.wait()
    pl.semaphore_wait(barrier, len(greeted))
    for quarter in range(2):
        for way in "+-":
            gather_z(way, 1, quarter)
    for way in "+-":
        gather_ids(way, 1)
    cw.wait()
    W[:LAB] = WF[...].astype(BF16)
    start(("cw",), W.at[pl.ds(0, LAB)], W.at[pl.ds(LAB, LAB)], partner)
    for i in range(SUB):
        start(("xw", "+", i), W.at[pl.ds(half + i * PIECE, PIECE)], W.at[pl.ds(2 * LAB + i * PIECE, PIECE)], x_of["+"])
        start(("xw", "-", i), W.at[pl.ds(i * PIECE, PIECE)], W.at[pl.ds(3 * LAB + i * PIECE, PIECE)], x_of["-"])
    build_mask(0)

    step_gather(1)
    build_mask(1)
    build_mask(7)
    forward_weights(0)
    step_gather(2)
    build_mask(2)
    build_mask(6)
    arrived(("cw",), *[("yg", s, k) for s in (1, 7) for k in range(2)])
    work(1, 0)
    forward_weights(1)
    step_gather(3)
    build_mask(3)
    build_mask(5)
    arrived(*[("yg", s, k) for s in (2, 6) for k in range(2)])
    work(2, 0)
    forward_weights(2)
    step_gather(4)
    build_mask(4)
    forward_weights(3)
    arrived(*[("yg", s, k) for s in (3, 5) for k in range(2)])
    work(3, 0)
    arrived(*[("yg", 4, k) for k in range(2)])
    work(4, 0)
    arrived(*[("fw", way, i) for way in "+-" for i in range(SUB)])
    work(4, 1)
    reduce_y(4)
    work(3, 1)
    reduce_y(3)
    reduce_y(5)
    reduce_z(1)
    work(2, 1)
    reduce_y(2)
    reduce_y(6)
    reduce_z(2)
    work(1, 1)
    reduce_y(1)
    reduce_y(7)
    reduce_y(0)

    for n, (way, base) in enumerate((("+", 2 * LAB), ("-", 3 * LAB))):
        for i in range(SUB):
            GCS[n, i] = WG[base + half + i * PIECE:base + half + (i + 1) * PIECE].astype(BF16)
            start(("gc", way, i), GCS.at[n, i], GCR.at[n, i], partner)
    for i in range(2):
        GOS[i] = WG[LAB + i * half:LAB + (i + 1) * half].astype(BF16)
        start(("go", i), GOS.at[i], GOR.at[i], partner)
    reduce_z(3)
    for i in range(SUB):
        for n, (way, base) in enumerate((("+", 2 * LAB), ("-", 3 * LAB))):
            arrived(("gc", way, i))
            GXS[n, i] = (WG[base + i * PIECE:base + (i + 1) * PIECE] + GCR[n, i].astype(F32)).astype(BF16)
            start(("gx", way, i), GXS.at[n, i], GXR.at[n, i], x_of["-" if way == "+" else "+"])
    reduce_z(4)
    for i in range(2):
        arrived(("go", i))
        WG[i * half:(i + 1) * half] += GOR[i].astype(F32)

    ry, rx = y // 2, xh
    mine = ry * 2 + rx
    done = {}
    sums = [total(0, quarter) for quarter in range(2)]
    for quarter in range(2):
        RS[quarter * QUARTER:(quarter + 1) * QUARTER] = sums[quarter]
    eighth = QB // 8
    for k in range(1, 4):
        owner = ((ry + k // 2) % 2) * 2 + (rx + k) % 2
        take = pl.ds(pl.multiple_of(owner * eighth, eighth), eighth)
        RR[0, k] = RS[take].astype(BF16)
        start(("rs", k), RR.at[0, k], RR.at[1, k], same[2 * (k // 2) * 2 + k % 2])
    for i in range(SUB):
        for n, (way, base) in enumerate((("+", half), ("-", 0))):
            arrived(("gx", way, i))
            wg_out[base + i * PIECE:base + (i + 1) * PIECE] = (
                WG[base + i * PIECE:base + (i + 1) * PIECE] + GXR[n, i].astype(F32)
            )
    t = RS[pl.ds(pl.multiple_of(mine * eighth, eighth), eighth)]
    for k in range(1, 4):
        arrived(("rs", k))
        t = t + RR[1, k].astype(F32)
    place = pl.ds(pl.multiple_of(p * (QB // 2) + mine * eighth, eighth), eighth)
    OUT[place] = t.astype(BF16)
    for k in range(1, 8):
        start(("ag", k), OUT.at[place], OUT.at[place], same[k])
    for k in range(1, 8):
        arrived(("ag", k))
    qg_out[...] = OUT[...]
    for cp in cps.values():
        cp.wait_send()


def step(queries, label_ids, weights):
    n = len(NAMES)
    vmem = pl.BlockSpec(memory_space=pltpu.VMEM)
    anywhere = pl.BlockSpec(memory_space=pl.ANY)
    tokens = ZN * QB
    labels = 4 * LAB
    return pl.pallas_call(
        kernel,
        out_shape=(jax.ShapeDtypeStruct((LAB, D), F32), jax.ShapeDtypeStruct((QB, D), BF16)),
        in_specs=[anywhere, vmem, anywhere],
        out_specs=(vmem, vmem),
        scratch_shapes=[
            pltpu.VMEM((tokens, D), BF16),
            pltpu.VMEM((8, LIST, QB), jnp.int32),
            pltpu.VMEM((tokens, 128), jnp.int32),
            pltpu.VMEM((LAB, D), F32),
            pltpu.VMEM((labels, D), BF16),
            pltpu.VMEM((labels, D), F32),
            pltpu.VMEM((tokens, D), F32),
            pltpu.VMEM((8, 2, QUARTER, D), BF16),
            pltpu.VMEM((8, 2, QUARTER, D), BF16),
            pltpu.VMEM((2, 4, 2, QUARTER, D), BF16),
            pltpu.VMEM((2, 4, 2, QUARTER, D), BF16),
            pltpu.VMEM((2, LAB // 2, D), BF16),
            pltpu.VMEM((2, LAB // 2, D), BF16),
            pltpu.VMEM((2, SUB, PIECE, D), BF16),
            pltpu.VMEM((2, SUB, PIECE, D), BF16),
            pltpu.VMEM((2, SUB, PIECE, D), BF16),
            pltpu.VMEM((2, SUB, PIECE, D), BF16),
            pltpu.VMEM((QB // 2, D), F32),
            pltpu.VMEM((2, 4, QB // 8, D), BF16),
            pltpu.VMEM((QB, D), BF16),
            pltpu.SemaphoreType.DMA((2,)),
            pltpu.SemaphoreType.DMA((n,)),
            pltpu.SemaphoreType.DMA((n,)),
        ],
        compiler_params=pltpu.CompilerParams(
            collective_id=0, has_side_effects=True, vmem_limit_bytes=56 * 1024 * 1024
        ),
        name="step",
    )(queries, label_ids, weights)


def body(queries, label_ids, weights, momentum):
    w_grad, q_grad = step(queries, label_ids, weights)
    new_momentum = keep_rate * momentum + w_grad
    new_weights = weights - step_rate * new_momentum
    return new_weights, new_momentum, q_grad.astype(F32)


def solution(mesh):
    return jax.shard_map(
        body,
        mesh=mesh,
        in_specs=(P("blk", None), P("blk", None), P(("blk", "cols"), None), P(("blk", "cols"), None)),
        out_specs=(P(("blk", "cols"), None), P(("blk", "cols"), None), P("blk", None)),
        check_vma=False,
    )
```

time: 348 us -> 71.6 us (0.21)
  the two profiles are of different devices: /device:TPU:1 before, /device:TPU:32 now
where the time goes in v1:
time: 71.6 us; the launch traced here: 71.4 us
  Pallas kernels  64.5 us (90%)
  other arithmetic  4.69 us (7%)
  local copies, waits for them, and re-layouts  1.54 us (2%)
    pallas_call x1, Pallas kernels, step(): pl.pallas_call(kernel, out_shape=(jax.ShapeDtypeStruct((LAB, D), F32), ja...  64.5 us
    sub x1, other arithmetic, body(): new_weights = weights - step_rate * new_momentum  3.92 us
    unnamed x5, local copies, waits for them, and re-layouts  1.54 us

profile of v1, /device:TPU:32, one launch (start us, length us, event | category | flops | bytes accessed | tf_op | source)
XLA Modules:
  0.0 71.4 jit_solution(14037475439021839723)
XLA Ops:
  0.6 0.0 copy-start
  0.6 1.5 %copy.7.ids_in = s32[128,8]{1,0:T(8,128)} copy(s32[128,8]{0,1:T(8,128)} %param.5) | data formatting | bytes 8192 | tf_op args[1]
  2.2 64.5 %step.1 = (f32[512,768]{1,0:T(8,128)}, bf16[128,768]{1,0:T(8,128)(2,1)}) custom-call(bf16[128,768]{1,0:T(8,128)(2,1)} %q_in.1, s32[128,8]{1,0:T(8,128)} %copy.7.ids_in, f32[512,768]{1,0:T(8,128)} %w_in.1), custom_call_target="tpu_custom_call" | custom-call | tf_op jit(solution)/shard_map/step/pallas_call | solution.py:335
  66.7 0.0 copy-done
  66.7 0.0 copy-start.1
  66.7 3.9 %multiply_subtract_fusion = (f32[512,768]{1,0:T(8,128)}, f32[512,768]{1,0:T(8,128)}) fusion(f32[512,768]{1,0:T(8,128)S(1)} %copy-done, f32[512,768]{1,0:T(8,128)} %get-tuple-element.5, f32[512,768]{1,0:T(8,128)} %param.7), kind=kLoop, calls=%fused_computation | loop fusion | flops 1572864 | bytes 7864320 | tf_op jit(solution)/shard_map/sub | solution.py:375
  70.6 0.0 copy-done.1
  70.6 0.8 %convert_element_type.3 = f32[128,768]{1,0:T(8,128)} convert(bf16[128,768]{1,0:T(8,128)(2,1)S(1)} %copy-done.1) | non-fusion elementwise | flops 98304 | bytes 589824 | tf_op jit(solution)/shard_map/convert_element_type | solution.py:376
Async XLA Ops:
  0.6 66.0 %copy-start = (f32[512,768]{1,0:T(8,128)S(1)}, f32[512,768]{1,0:T(8,128)}, u32[]{:S(2)}) copy-start(f32[512,768]{1,0:T(8,128)} %w_in.1) | copy-start | bytes 4718596
  66.7 3.9 %copy-start.1 = (bf16[128,768]{1,0:T(8,128)(2,1)S(1)}, bf16[128,768]{1,0:T(8,128)(2,1)}, u32[]{:S(2)}) copy-start(bf16[128,768]{1,0:T(8,128)(2,1)} %get-tuple-element.6) | copy-start | bytes 589828

commit v2 on v1

v2 whole, which is shorter than its diff:
```python
import functools

import jax
import jax.numpy as jnp
from jax import lax
from jax.experimental import pallas as pl
from jax.experimental.pallas import tpu as pltpu
from jax.sharding import PartitionSpec as P

MESH = pl.DeviceIdType.MESH
F32, BF16 = jnp.float32, jnp.bfloat16
NT = (((1,), (1,)), ((), ()))
TN = (((0,), (0,)), ((), ()))
NN = (((1,), (0,)), ((), ()))

loss_scale = 1.0 / 16.0
keep_rate = 0.9
step_rate = 0.005

D = 768
LAB = 512
QB = 128
ZN, YN, XN = 8, 4, 4
LIST = 8
SUB = 4
PIECE = LAB // 2 // SUB
PLACE = {1: 0, 7: 1, 2: 2, 6: 3, 3: 4, 5: 5, 4: 6, 0: 7}
QUARTER = QB // 4


def dot(a, b, dims):
    return lax.dot_general(a, b, dims, preferred_element_type=F32)


def device(z, y, x, core):
    return (z * 4 + (x % 2) * 2 + core, y * 2 + x // 2)


TOWARDS = {3: 2, 2: 1, 1: 0, 5: 6, 6: 7, 7: 0}
PARTS = {slot: 3 if slot == 4 else 2 for slot in range(8)}


def copy_names():
    names = [("zg", r, k) for r in range(1, 8) for k in range(2)] + [("id", r) for r in range(1, 8)]
    names += [("yg", r, k) for r in range(1, 8) for k in range(2)]
    names += [("cw",)]
    names += [(kind, way, i) for kind in ("xw", "fw", "gc", "gx") for way in "+-" for i in range(SUB)]
    names += [("go", i) for i in range(2)]
    names += [("yr", r, k) for r in range(8) for k in range(PARTS[r])]
    names += [("zr", r, k) for r in (3, 2, 5, 6) for k in range(2)]
    names += [("zl", r, m) for r in (0, 1, 7, 4) for m in range(2 if r == 4 else 4) if r or m]
    names += [("ag", k) for k in range(1, 8)]
    return names


NAMES = {name: i for i, name in enumerate(copy_names())}


def kernel(
    q_in, ids_in, w_in, wg_out, qg_out,
    Q, IDS, M, WF, W, WG, QG, YS, YR, ZS, ZR, GOS, GOR, GCS, GCR, GXS, GXR, LS, LR, OWN, OUT, local_sem, send_sem, recv_sem,
):
    blk, cols = lax.axis_index("blk"), lax.axis_index("cols")
    z, xl, core = blk // 4, (blk // 2) % 2, blk % 2
    y, xh = cols // 2, cols % 2
    x = xh * 2 + xl
    p = y % 2

    s = y // 2
    z_of = {r: device((z + r) % ZN, y, x, core) for r in range(1, 8)}
    y_of = {k: device(z, (y + k) % YN, x, core) for k in (1, 2, 3)}
    x_of = {"+": device(z, y, (x + 1) % XN, core), "-": device(z, y, (x + XN - 1) % XN, core)}
    partner = device(z, y, x, 1 - core)
    far_x = (x + 2) % XN
    same = {k: device(z, (y + k // 2) % YN, far_x if k % 2 else x, core) for k in range(1, 8)}

    cq = pltpu.make_async_copy(q_in, Q.at[pl.ds(PLACE[0] * QB, QB)], local_sem.at[0])
    cq.start()
    cw = pltpu.make_async_copy(w_in, WF, local_sem.at[1])
    cw.start()

    barrier = pltpu.get_barrier_semaphore()
    def owner(r, m):
        return device((z + r) % ZN, (y + 2 * (m // 2)) % YN, far_x if m % 2 else x, core)

    greeted = [partner] + list(x_of.values()) + list(same.values())
    greeted += [owner(r, m) for r in (1, 7) for m in range(4)] + [owner(4, 0), owner(4, 1)]
    for d in greeted:
        pl.semaphore_signal(barrier, inc=1, device_id=d, device_id_type=MESH)

    IDS[0] = ids_in[...]

    cps = {}

    def start(name, src, dst, dev):
        cp = pltpu.make_async_remote_copy(
            src_ref=src, dst_ref=dst, send_sem=send_sem.at[NAMES[name]], recv_sem=recv_sem.at[NAMES[name]],
            device_id=dev, device_id_type=MESH,
        )
        cp.start()
        cps[name] = cp

    def arrived(*names):
        for name in names:
            cps[name].wait_recv()

    def rows(slot, half, quarter, count=QUARTER):
        return pl.ds(pl.multiple_of(PLACE[slot] * QB + half * (QB // 2) + quarter * QUARTER, QUARTER), count)

    def gather_z(slot, k, src):
        start(("zg", slot, k), Q.at[rows(src, p, k)], Q.at[rows(slot, p, k)], z_of[7 if src < 4 and slot == src + 1 else 1])

    def gather_ids(slot):
        src = TOWARDS[slot]
        if src:
            arrived(("id", src))
        start(("id", slot), IDS.at[src], IDS.at[slot], z_of[7 if slot < 4 else 1])

    def gather_step(step, k):
        for slot in (8 - step, step) if step < 4 else (4,):
            arrived(("zg", slot, k))
            if step < 3:
                gather_z(slot - 1 if slot > 4 else slot + 1, k, slot)
            elif step == 3 and slot == (5, 3)[k]:
                gather_z(4, k, slot)
            here = Q.at[rows(slot, p, k)]
            start(("yg", slot, k), here, here, y_of[1 + 2 * k])

    def gathered(*slots):
        for slot in slots:
            arrived(("yg", slot, 0), ("yg", slot, 1))

    def forward_weights(i):
        for way, base in (("+", 2 * LAB), ("-", 3 * LAB)):
            arrived(("xw", way, i))
            start(("fw", way, i), W.at[pl.ds(base + i * PIECE, PIECE)],
                  W.at[pl.ds(base + LAB // 2 + i * PIECE, PIECE)], partner)

    def first(z, y, x, core):
        b, c = device(z, y, x, core)
        return (b * 8 + c) * LAB

    left, right = (x + XN - 1) % XN, (x + 1) % XN
    half = LAB // 2
    pieces = [
        (0, LAB, first(z, y, x, core)),
        (LAB, LAB, first(z, y, x, 1 - core)),
        (2 * LAB, half, first(z, y, left, core) + half),
        (2 * LAB + half, half, first(z, y, left, 1 - core) + half),
        (3 * LAB, half, first(z, y, right, core)),
        (3 * LAB + half, half, first(z, y, right, 1 - core)),
    ]

    def build_mask(slot):
        ids = IDS[slot]
        row = jnp.full(ids.shape, -1, jnp.int32)
        for base, count, label in pieces:
            local = ids - label
            row = jnp.where((local >= 0) & (local < count), local + base, row)
        low = jnp.where(row >= 0, row % 128, -1)
        bit = jnp.left_shift(1, jnp.maximum(row, 0) // 128)
        sub = lax.broadcasted_iota(jnp.int32, (128, QB), 0)
        m = jnp.zeros((128, QB), jnp.int32)
        for j in range(LIST):
            m = m | jnp.where(low[j:j + 1] == sub, bit[j:j + 1], 0)
        M[PLACE[slot] * QB:(PLACE[slot] + 1) * QB] = jnp.transpose(m)

    seen = set()

    def work(slot, part):
        at = PLACE[slot] * QB
        here, there = slice(at, at + 2 * QB), slice(part * 2 * LAB, (part + 1) * 2 * LAB)
        q, w, m = Q[here], W[there], M[here]
        scores = dot(q, w, NT)
        out = []
        for b in range(2 * LAB // 128):
            target = ((m >> (part * 2 * LAB // 128 + b)) & 1).astype(F32)
            out.append(((jax.nn.sigmoid(scores[:, b * 128:(b + 1) * 128]) - target) * loss_scale).astype(BF16))
        grad = jnp.concatenate(out, axis=1)
        a = dot(grad, w, NN)
        if (slot,) not in seen:
            QG[here] = a
        else:
            QG[here] += a
        g = dot(grad, q, TN)
        if part not in seen:
            WG[there] = g
        else:
            WG[there] += g
        seen.update([part, (slot,)])

    def reduce_y(slot):
        for k in range(PARTS[slot]):
            if slot == 4:
                there = (y + k + 1) % YN
                YS[slot, k] = QG[rows(slot, there % 2, there // 2)].astype(BF16)
                start(("yr", slot, k), YS.at[slot, k], YR.at[slot, k], y_of[k + 1])
            else:
                YS[slot, k] = QG[rows(slot, 1 - p, k)].astype(BF16)
                start(("yr", slot, k), YS.at[slot, k], YR.at[slot, k], y_of[3 - 2 * k])

    def eighth(which):
        return pl.ds(pl.multiple_of(which * (QB // 8), QB // 8), QB // 8)

    def total(slot, k):
        arrived(("yr", slot, k))
        t = QG[rows(slot, p, k)] + YR[slot, k].astype(F32)
        before = {2: 3, 1: 2, 6: 5, 7: 6}.get(slot)
        if before:
            arrived(("zr", before, k))
            t = t + ZR[slot, k].astype(F32)
        return t

    def reduce_z(slot):
        for k in range(2):
            ZS[slot, k] = total(slot, k).astype(BF16)
            start(("zr", slot, k), ZS.at[slot, k], ZR.at[TOWARDS[slot], k], z_of[1 if slot < 4 else 7])

    def reduce_last(slot):
        if slot == 4:
            arrived(*[("yr", 4, k) for k in range(3)])
            t = QG[rows(4, p, s)]
            for k in range(3):
                t = t + YR[4, k].astype(F32)
            LS[4, :QUARTER] = t.astype(BF16)
        else:
            for k in range(2):
                t = total(slot, k)
                LS[slot, k * QUARTER:(k + 1) * QUARTER] = t.astype(BF16)
                if slot == 0:
                    OWN[k * QUARTER:(k + 1) * QUARTER] = t
        for m in range(4):
            if ("zl", slot, m) in NAMES:
                j = (xh + m) % 2
                part = eighth(j if slot == 4 else (s + m // 2) % 2 * 2 + j)
                start(("zl", slot, m), LS.at[slot, part], LR.at[slot, m], owner(slot, m))

    cq.wait()
    pl.semaphore_wait(barrier, len(greeted))
    for slot in (7, 1):
        gather_z(slot, 0, 0)
    gather_ids(1)
    gather_ids(7)
    start(("id", 4), IDS.at[0], IDS.at[4], z_of[4])
    cw.wait()
    W[:LAB] = WF[...].astype(BF16)
    for slot in (7, 1):
        gather_z(slot, 1, 0)
    start(("cw",), W.at[pl.ds(0, LAB)], W.at[pl.ds(LAB, LAB)], partner)
    for i in range(SUB):
        start(("xw", "+", i), W.at[pl.ds(half + i * PIECE, PIECE)], W.at[pl.ds(2 * LAB + i * PIECE, PIECE)], x_of["+"])
        start(("xw", "-", i), W.at[pl.ds(i * PIECE, PIECE)], W.at[pl.ds(3 * LAB + i * PIECE, PIECE)], x_of["-"])
    build_mask(0)
    gather_step(1, 0)
    gather_ids(2)
    gather_ids(6)
    gather_step(1, 1)
    build_mask(1)
    build_mask(7)
    gather_step(2, 0)
    forward_weights(0)
    gather_ids(3)
    gather_ids(5)
    gather_step(2, 1)
    arrived(("cw",))
    gathered(1, 7)
    work(1, 0)
    gather_step(3, 0)
    forward_weights(1)
    build_mask(2)
    build_mask(6)
    gather_step(3, 1)
    forward_weights(2)
    arrived(("id", 4), ("id", 3), ("id", 5))
    gathered(2, 6)
    work(2, 0)
    forward_weights(3)
    gather_step(4, 0)
    gather_step(4, 1)
    for slot in (3, 5, 4):
        build_mask(slot)
    gathered(3, 5)
    work(3, 0)
    arrived(*[("fw", way, i) for way in "+-" for i in range(SUB)])
    work(3, 1)
    reduce_y(3)
    reduce_y(5)
    gathered(4)
    work(4, 0)
    work(4, 1)
    reduce_y(4)
    reduce_y(0)
    reduce_z(3)
    reduce_z(5)
    work(2, 1)
    reduce_y(2)
    reduce_y(6)
    reduce_last(4)
    reduce_last(0)
    work(1, 1)
    reduce_y(1)
    reduce_y(7)
    for n, (way, base) in enumerate((("+", 2 * LAB), ("-", 3 * LAB))):
        for i in range(SUB):
            GCS[n, i] = WG[base + half + i * PIECE:base + half + (i + 1) * PIECE].astype(BF16)
            start(("gc", way, i), GCS.at[n, i], GCR.at[n, i], partner)
    reduce_z(2)
    reduce_z(6)
    for i in range(SUB):
        for n, (way, base) in enumerate((("+", 2 * LAB), ("-", 3 * LAB))):
            arrived(("gc", way, i))
            GXS[n, i] = (WG[base + i * PIECE:base + (i + 1) * PIECE] + GCR[n, i].astype(F32)).astype(BF16)
            start(("gx", way, i), GXS.at[n, i], GXR.at[n, i], x_of["-" if way == "+" else "+"])
    for i in range(2):
        GOS[i] = WG[LAB + i * half:LAB + (i + 1) * half].astype(BF16)
        start(("go", i), GOS.at[i], GOR.at[i], partner)
    reduce_last(1)
    reduce_last(7)
    for i in range(2):
        arrived(("go", i))
        WG[i * half:(i + 1) * half] += GOR[i].astype(F32)

    t = OWN[eighth(s * 2 + xh)]
    for slot in (4, 0, 1, 7):
        for m in range(4):
            if ("zl", slot, m) in NAMES:
                arrived(("zl", slot, m))
                t = t + LR[slot, m].astype(F32)
    place = eighth(p * 4 + s * 2 + xh)
    OUT[place] = t.astype(BF16)
    for k in range(1, 8):
        start(("ag", k), OUT.at[place], OUT.at[place], same[k])
    for i in range(SUB):
        for n, (way, base) in enumerate((("+", half), ("-", 0))):
            arrived(("gx", way, i))
            wg_out[base + i * PIECE:base + (i + 1) * PIECE] = (
                WG[base + i * PIECE:base + (i + 1) * PIECE] + GXR[n, i].astype(F32)
            )
    for k in range(1, 8):
        arrived(("ag", k))
    qg_out[...] = OUT[...]
    for cp in cps.values():
        cp.wait_send()


def step(queries, label_ids, weights):
    n = len(NAMES)
    vmem = pl.BlockSpec(memory_space=pltpu.VMEM)
    anywhere = pl.BlockSpec(memory_space=pl.ANY)
    tokens = ZN * QB
    labels = 4 * LAB
    return pl.pallas_call(
        kernel,
        out_shape=(jax.ShapeDtypeStruct((LAB, D), F32), jax.ShapeDtypeStruct((QB, D), BF16)),
        in_specs=[anywhere, vmem, anywhere],
        out_specs=(vmem, vmem),
        scratch_shapes=[
            pltpu.VMEM((tokens, D), BF16),
            pltpu.VMEM((8, LIST, QB), jnp.int32),
            pltpu.VMEM((tokens, 128), jnp.int32),
            pltpu.VMEM((LAB, D), F32),
            pltpu.VMEM((labels, D), BF16),
            pltpu.VMEM((labels, D), F32),
            pltpu.VMEM((tokens, D), F32),
            pltpu.VMEM((8, 3, QUARTER, D), BF16),
            pltpu.VMEM((8, 3, QUARTER, D), BF16),
            pltpu.VMEM((8, 2, QUARTER, D), BF16),
            pltpu.VMEM((8, 2, QUARTER, D), BF16),
            pltpu.VMEM((2, LAB // 2, D), BF16),
            pltpu.VMEM((2, LAB // 2, D), BF16),
            pltpu.VMEM((2, SUB, PIECE, D), BF16),
            pltpu.VMEM((2, SUB, PIECE, D), BF16),
            pltpu.VMEM((2, SUB, PIECE, D), BF16),
            pltpu.VMEM((2, SUB, PIECE, D), BF16),
            pltpu.VMEM((8, QB // 2, D), BF16),
            pltpu.VMEM((8, 4, QB // 8, D), BF16),
            pltpu.VMEM((QB // 2, D), F32),
            pltpu.VMEM((QB, D), BF16),
            pltpu.SemaphoreType.DMA((2,)),
            pltpu.SemaphoreType.DMA((n,)),
            pltpu.SemaphoreType.DMA((n,)),
        ],
        compiler_params=pltpu.CompilerParams(
            collective_id=0, has_side_effects=True, vmem_limit_bytes=40 * 1024 * 1024
        ),
        name="step",
    )(queries, label_ids, weights)


def body(queries, label_ids, weights, momentum):
    w_grad, q_grad = step(queries, label_ids.T, weights)
    new_momentum = keep_rate * momentum + w_grad
    new_weights = weights - step_rate * new_momentum
    return new_weights, new_momentum, q_grad.astype(F32)


def solution(mesh):
    return jax.shard_map(
        body,
        mesh=mesh,
        in_specs=(P("blk", None), P("blk", None), P(("blk", "cols"), None), P(("blk", "cols"), None)),
        out_specs=(P(("blk", "cols"), None), P(("blk", "cols"), None), P("blk", None)),
        check_vma=False,
    )
```

time: 71.6 us -> 65.9 us (0.920)
  the two profiles are of different devices: /device:TPU:32 before, /device:TPU:1 now
where the time goes in v2:
time: 65.9 us; the launch traced here: 65.8 us
  Pallas kernels  59.3 us (90%)
  local copies, waits for them, and re-layouts  3.02 us (5%)
  other arithmetic  2.77 us (4%)
  between operations  0.66 us (1%)
    pallas_call x1, Pallas kernels, step(): pl.pallas_call(kernel, out_shape=(jax.ShapeDtypeStruct((LAB, D), F32), ja...  59.3 us
    unnamed x8, local copies, waits for them, and re-layouts  3.02 us
    sub x1, other arithmetic, body(): new_weights = weights - step_rate * new_momentum  2 us

profile of v2, /device:TPU:1, one launch (start us, length us, event | category | flops | bytes accessed | tf_op | source)
XLA Modules:
  0.0 65.8 jit_solution(328985422059718578)
XLA Ops:
  0.6 0.0 copy-start
  0.6 1.4 %copy-done = f32[512,768]{1,0:T(8,128)S(1)} copy-done((f32[512,768]{1,0:T(8,128)S(1)}, f32[512,768]{1,0:T(8,128)}, u32[]{:S(2)}) %copy-start) | copy-done | bytes 1572888
  2.0 0.0 copy-start.1
  2.0 0.9 %copy-done.1 = bf16[128,768]{1,0:T(8,128)(2,1)S(1)} copy-done((bf16[128,768]{1,0:T(8,128)(2,1)S(1)}, bf16[128,768]{1,0:T(8,128)(2,1)}, u32[]{:S(2)}) %copy-start.1) | copy-done | bytes 196632
  3.0 0.0 copy-start.2
  3.0 0.7 %copy-done.2 = s32[128,8]{0,1:T(8,128)S(1)} copy-done((s32[128,8]{0,1:T(8,128)S(1)}, s32[128,8]{0,1:T(8,128)}, u32[]{:S(2)}) %copy-start.2) | copy-done | bytes 4120
  3.7 0.0 copy-start.3
  3.7 59.3 %step.1 = (f32[512,768]{1,0:T(8,128)S(1)}, bf16[128,768]{1,0:T(8,128)(2,1)S(1)}) custom-call(bf16[128,768]{1,0:T(8,128)(2,1)S(1)} %copy-done.1, s32[8,128]{1,0:T(8,128)S(1)} %bitcast.1, f32[512,768]{1,0:T(8,128)S(1)} %copy-done), custom_call_target="tpu_custom_call" | custom-call | tf_op jit(solution)/shard_map/step/pallas_call | solution.py:352
  63.0 0.0 copy-done.3
  63.0 2.0 %multiply_subtract_fusion = (f32[512,768]{1,0:T(8,128)}, f32[512,768]{1,0:T(8,128)}) fusion(f32[512,768]{1,0:T(8,128)S(1)} %copy-done, f32[512,768]{1,0:T(8,128)S(1)} %get-tuple-element.5, f32[512,768]{1,0:T(8,128)S(1)} %copy-done.3), kind=kLoop, calls=%fused_computation | loop fusion | flops 1572864 | bytes 7864320 | tf_op jit(solution)/shard_map/sub | solution.py:393
  65.0 0.8 %convert_element_type.3 = f32[128,768]{1,0:T(8,128)} convert(bf16[128,768]{1,0:T(8,128)(2,1)S(1)} %get-tuple-element.6) | non-fusion elementwise | flops 98304 | bytes 589824 | tf_op jit(solution)/shard_map/convert_element_type | solution.py:394
Async XLA Ops:
  0.6 1.4 %copy-start = (f32[512,768]{1,0:T(8,128)S(1)}, f32[512,768]{1,0:T(8,128)}, u32[]{:S(2)}) copy-start(f32[512,768]{1,0:T(8,128)} %w_in.1) | copy-start | bytes 4718596
  2.0 0.9 %copy-start.1 = (bf16[128,768]{1,0:T(8,128)(2,1)S(1)}, bf16[128,768]{1,0:T(8,128)(2,1)}, u32[]{:S(2)}) copy-start(bf16[128,768]{1,0:T(8,128)(2,1)} %q_in.1) | copy-start | bytes 589828
  3.0 0.7 %copy-start.2 = (s32[128,8]{0,1:T(8,128)S(1)}, s32[128,8]{0,1:T(8,128)}, u32[]{:S(2)}) copy-start(s32[128,8]{0,1:T(8,128)} %param.5) | copy-start | bytes 12292
  3.7 59.3 %copy-start.3 = (f32[512,768]{1,0:T(8,128)S(1)}, f32[512,768]{1,0:T(8,128)}, u32[]{:S(2)}) copy-start(f32[512,768]{1,0:T(8,128)} %param.7) | copy-start | bytes 4718596

commit v3 on v2

--- a/solution.py
+++ b/solution.py
@@ -53,7 +53,21 @@
     return names
 
 
-NAMES = {name: i for i, name in enumerate(copy_names())}
+NAMES = copy_names()
+ROWS = {"zg": QUARTER, "yg": QUARTER, "cw": LAB, "xw": PIECE, "fw": PIECE, "gc": PIECE, "gx": PIECE, "go": LAB // 2,
+        "yr": QUARTER, "zr": QUARTER, "zl": QB // 8, "ag": QB // 8, "id": 0}
+
+
+def group(name):
+    if name[0] in ("fw", "ag"):
+        return name[:1]
+    if name[0] in ("yg", "zl") or name[:2] == ("yr", 4):
+        return name[:2]
+    return name
+
+
+GROUPS = list(dict.fromkeys(group(name) for name in NAMES))
+KINDS = list(ROWS)
 
 
 def kernel(
@@ -76,6 +90,8 @@
 
     cq = pltpu.make_async_copy(q_in, Q.at[pl.ds(PLACE[0] * QB, QB)], local_sem.at[0])
     cq.start()
+    ci = pltpu.make_async_copy(ids_in, IDS.at[0], local_sem.at[2])
+    ci.start()
     cw = pltpu.make_async_copy(w_in, WF, local_sem.at[1])
     cw.start()
 
@@ -88,21 +104,39 @@
     for d in greeted:
         pl.semaphore_signal(barrier, inc=1, device_id=d, device_id_type=MESH)
 
-    IDS[0] = ids_in[...]
-
-    cps = {}
+
+    started, waited = [], set()
 
     def start(name, src, dst, dev):
+        pltpu.make_async_remote_copy(
+            src_ref=src, dst_ref=dst, send_sem=send_sem.at[KINDS.index(name[0])],
+            recv_sem=recv_sem.at[GROUPS.index(group(name))], device_id=dev, device_id_type=MESH,
+        ).start()
+        started.append(name)
+
+    def await_bytes(names, index, sent):
+        if names[0][0] == "id":
+            ref = IDS.at[pl.ds(0, len(names))]
+        else:
+            ref = W.at[pl.ds(0, sum(ROWS[name[0]] for name in names))]
         cp = pltpu.make_async_remote_copy(
-            src_ref=src, dst_ref=dst, send_sem=send_sem.at[NAMES[name]], recv_sem=recv_sem.at[NAMES[name]],
-            device_id=dev, device_id_type=MESH,
+            src_ref=ref, dst_ref=ref, send_sem=send_sem.at[index if sent else 0], recv_sem=recv_sem.at[0 if sent else index],
+            device_id=partner, device_id_type=MESH,
         )
-        cp.start()
-        cps[name] = cp
+        if sent:
+            cp.wait_send()
+        else:
+            cp.wait_recv()
 
     def arrived(*names):
-        for name in names:
-            cps[name].wait_recv()
+        for key in dict.fromkeys(group(name) for name in names):
+            if key not in waited:
+                waited.add(key)
+                await_bytes([name for name in NAMES if group(name) == key], GROUPS.index(key), False)
+
+    def sent(*kinds):
+        for kind in kinds:
+            await_bytes([name for name in started if name[0] == kind], KINDS.index(kind), True)
 
     def rows(slot, half, quarter, count=QUARTER):
         return pl.ds(pl.multiple_of(PLACE[slot] * QB + half * (QB // 2) + quarter * QUARTER, QUARTER), count)
@@ -229,7 +263,7 @@
                 LS[slot, k * QUARTER:(k + 1) * QUARTER] = t.astype(BF16)
                 if slot == 0:
                     OWN[k * QUARTER:(k + 1) * QUARTER] = t
-        for m in range(4):
+        for m in (3, 2, 1, 0):
             if ("zl", slot, m) in NAMES:
                 j = (xh + m) % 2
                 part = eighth(j if slot == 4 else (s + m // 2) % 2 * 2 + j)
@@ -239,6 +273,7 @@
     pl.semaphore_wait(barrier, len(greeted))
     for slot in (7, 1):
         gather_z(slot, 0, 0)
+    ci.wait()
     gather_ids(1)
     gather_ids(7)
     start(("id", 4), IDS.at[0], IDS.at[4], z_of[4])
@@ -270,42 +305,43 @@
     build_mask(2)
     build_mask(6)
     gather_step(3, 1)
-    forward_weights(2)
-    arrived(("id", 4), ("id", 3), ("id", 5))
     gathered(2, 6)
     work(2, 0)
+    forward_weights(2)
     forward_weights(3)
+    arrived(("id", 4), ("id", 3), ("id", 5))
+    build_mask(3)
+    build_mask(5)
     gather_step(4, 0)
     gather_step(4, 1)
-    for slot in (3, 5, 4):
-        build_mask(slot)
+    build_mask(4)
     gathered(3, 5)
     work(3, 0)
     arrived(*[("fw", way, i) for way in "+-" for i in range(SUB)])
     work(3, 1)
     reduce_y(3)
     reduce_y(5)
+    work(2, 1)
+    reduce_y(2)
+    reduce_y(6)
     gathered(4)
     work(4, 0)
+    reduce_z(3)
+    reduce_z(5)
     work(4, 1)
     reduce_y(4)
     reduce_y(0)
-    reduce_z(3)
-    reduce_z(5)
-    work(2, 1)
-    reduce_y(2)
-    reduce_y(6)
-    reduce_last(4)
-    reduce_last(0)
     work(1, 1)
     reduce_y(1)
     reduce_y(7)
+    reduce_z(2)
+    reduce_z(6)
+    reduce_last(4)
+    reduce_last(0)
     for n, (way, base) in enumerate((("+", 2 * LAB), ("-", 3 * LAB))):
         for i in range(SUB):
             GCS[n, i] = WG[base + half + i * PIECE:base + half + (i + 1) * PIECE].astype(BF16)
             start(("gc", way, i), GCS.at[n, i], GCR.at[n, i], partner)
-    reduce_z(2)
-    reduce_z(6)
     for i in range(SUB):
         for n, (way, base) in enumerate((("+", 2 * LAB), ("-", 3 * LAB))):
             arrived(("gc", way, i))
@@ -328,7 +364,7 @@
                 t = t + LR[slot, m].astype(F32)
     place = eighth(p * 4 + s * 2 + xh)
     OUT[place] = t.astype(BF16)
-    for k in range(1, 8):
+    for k in (5, 3, 7, 4, 1, 2, 6):
         start(("ag", k), OUT.at[place], OUT.at[place], same[k])
     for i in range(SUB):
         for n, (way, base) in enumerate((("+", half), ("-", 0))):
@@ -336,23 +372,21 @@
             wg_out[base + i * PIECE:base + (i + 1) * PIECE] = (
                 WG[base + i * PIECE:base + (i + 1) * PIECE] + GXR[n, i].astype(F32)
             )
-    for k in range(1, 8):
-        arrived(("ag", k))
+    sent(*[kind for kind in KINDS if kind != "ag"])
+    arrived(("ag", 1))
     qg_out[...] = OUT[...]
-    for cp in cps.values():
-        cp.wait_send()
+    sent("ag")
 
 
 def step(queries, label_ids, weights):
-    n = len(NAMES)
     vmem = pl.BlockSpec(memory_space=pltpu.VMEM)
-    anywhere = pl.BlockSpec(memory_space=pl.ANY)
+    hbm = pl.BlockSpec(memory_space=pltpu.HBM)
     tokens = ZN * QB
     labels = 4 * LAB
     return pl.pallas_call(
         kernel,
         out_shape=(jax.ShapeDtypeStruct((LAB, D), F32), jax.ShapeDtypeStruct((QB, D), BF16)),
-        in_specs=[anywhere, vmem, anywhere],
+        in_specs=[hbm, hbm, hbm],
         out_specs=(vmem, vmem),
         scratch_shapes=[
             pltpu.VMEM((tokens, D), BF16),
@@ -376,9 +410,9 @@
             pltpu.VMEM((8, 4, QB // 8, D), BF16),
             pltpu.VMEM((QB // 2, D), F32),
             pltpu.VMEM((QB, D), BF16),
-            pltpu.SemaphoreType.DMA((2,)),
-            pltpu.SemaphoreType.DMA((n,)),
-            pltpu.SemaphoreType.DMA((n,)),
+            pltpu.SemaphoreType.DMA((3,)),
+            pltpu.SemaphoreType.DMA((len(KINDS),)),
+            pltpu.SemaphoreType.DMA((len(GROUPS),)),
         ],
         compiler_params=pltpu.CompilerParams(
             collective_id=0, has_side_effects=True, vmem_limit_bytes=40 * 1024 * 1024

time: 65.9 us -> 64.6 us (0.980)
  Pallas kernels: 59.3 us -> 58 us
    pallas_call x1, Pallas kernels: 59.3 us -> 58 us  [step(): pl.pallas_call(kernel, out_shape=(jax.ShapeDtypeStruct((LAB, D), F32), ja...]
where the time goes in v3:
time: 64.6 us; the launch traced here: 64.4 us
  Pallas kernels  58 us (90%)
  local copies, waits for them, and re-layouts  3.02 us (5%)
  other arithmetic  2.77 us (4%)
  between operations  0.66 us (1%)
    pallas_call x1, Pallas kernels, step(): pl.pallas_call(kernel, out_shape=(jax.ShapeDtypeStruct((LAB, D), F32), ja...  58 us
    unnamed x8, local copies, waits for them, and re-layouts  3.02 us
    sub x1, other arithmetic, body(): new_weights = weights - step_rate * new_momentum  2 us

profile of v3, /device:TPU:1, one launch (start us, length us, event | category | flops | bytes accessed | tf_op | source)
XLA Modules:
  0.0 64.4 jit_solution(5193486437583477614)
XLA Ops:
  0.6 0.0 copy-start
  0.6 1.4 %copy-done = f32[512,768]{1,0:T(8,128)S(1)} copy-done((f32[512,768]{1,0:T(8,128)S(1)}, f32[512,768]{1,0:T(8,128)}, u32[]{:S(2)}) %copy-start) | copy-done | bytes 1572888
  2.0 0.0 copy-start.1
  2.0 0.9 %copy-done.1 = bf16[128,768]{1,0:T(8,128)(2,1)S(1)} copy-done((bf16[128,768]{1,0:T(8,128)(2,1)S(1)}, bf16[128,768]{1,0:T(8,128)(2,1)}, u32[]{:S(2)}) %copy-start.1) | copy-done | bytes 196632
  3.0 0.0 copy-start.2
  3.0 0.7 %copy-done.2 = s32[128,8]{0,1:T(8,128)S(1)} copy-done((s32[128,8]{0,1:T(8,128)S(1)}, s32[128,8]{0,1:T(8,128)}, u32[]{:S(2)}) %copy-start.2) | copy-done | bytes 4120
  3.7 0.0 copy-start.3
  3.7 58.0 %step.1 = (f32[512,768]{1,0:T(8,128)S(1)}, bf16[128,768]{1,0:T(8,128)(2,1)S(1)}) custom-call(bf16[128,768]{1,0:T(8,128)(2,1)S(1)} %copy-done.1, s32[8,128]{1,0:T(8,128)S(1)} %bitcast.1, f32[512,768]{1,0:T(8,128)S(1)} %copy-done), custom_call_target="tpu_custom_call" | custom-call | tf_op jit(solution)/shard_map/step/pallas_call | solution.py:386
  61.7 0.0 copy-done.3
  61.7 2.0 %multiply_subtract_fusion = (f32[512,768]{1,0:T(8,128)}, f32[512,768]{1,0:T(8,128)}) fusion(f32[512,768]{1,0:T(8,128)S(1)} %copy-done, f32[512,768]{1,0:T(8,128)S(1)} %get-tuple-element.5, f32[512,768]{1,0:T(8,128)S(1)} %copy-done.3), kind=kLoop, calls=%fused_computation | loop fusion | flops 1572864 | bytes 7864320 | tf_op jit(solution)/shard_map/sub | solution.py:427
  63.7 0.8 %convert_element_type.3 = f32[128,768]{1,0:T(8,128)} convert(bf16[128,768]{1,0:T(8,128)(2,1)S(1)} %get-tuple-element.6) | non-fusion elementwise | flops 98304 | bytes 589824 | tf_op jit(solution)/shard_map/convert_element_type | solution.py:428
Async XLA Ops:
  0.6 1.4 %copy-start = (f32[512,768]{1,0:T(8,128)S(1)}, f32[512,768]{1,0:T(8,128)}, u32[]{:S(2)}) copy-start(f32[512,768]{1,0:T(8,128)} %w_in.1) | copy-start | bytes 4718596
  2.0 0.9 %copy-start.1 = (bf16[128,768]{1,0:T(8,128)(2,1)S(1)}, bf16[128,768]{1,0:T(8,128)(2,1)}, u32[]{:S(2)}) copy-start(bf16[128,768]{1,0:T(8,128)(2,1)} %q_in.1) | copy-start | bytes 589828
  3.0 0.7 %copy-start.2 = (s32[128,8]{0,1:T(8,128)S(1)}, s32[128,8]{0,1:T(8,128)}, u32[]{:S(2)}) copy-start(s32[128,8]{0,1:T(8,128)} %param.5) | copy-start | bytes 12292
  3.7 58.0 %copy-start.3 = (f32[512,768]{1,0:T(8,128)S(1)}, f32[512,768]{1,0:T(8,128)}, u32[]{:S(2)}) copy-start(f32[512,768]{1,0:T(8,128)} %param.7) | copy-start | bytes 4718596

commit v4 on v3

--- a/solution.py
+++ b/solution.py
@@ -334,14 +334,14 @@
     work(1, 1)
     reduce_y(1)
     reduce_y(7)
+    for n, (way, base) in enumerate((("+", 2 * LAB), ("-", 3 * LAB))):
+        for i in range(SUB):
+            GCS[n, i] = WG[base + half + i * PIECE:base + half + (i + 1) * PIECE].astype(BF16)
+            start(("gc", way, i), GCS.at[n, i], GCR.at[n, i], partner)
     reduce_z(2)
     reduce_z(6)
     reduce_last(4)
     reduce_last(0)
-    for n, (way, base) in enumerate((("+", 2 * LAB), ("-", 3 * LAB))):
-        for i in range(SUB):
-            GCS[n, i] = WG[base + half + i * PIECE:base + half + (i + 1) * PIECE].astype(BF16)
-            start(("gc", way, i), GCS.at[n, i], GCR.at[n, i], partner)
     for i in range(SUB):
         for n, (way, base) in enumerate((("+", 2 * LAB), ("-", 3 * LAB))):
             arrived(("gc", way, i))

time: 64.6 us -> 61.7 us (0.955)
  Pallas kernels: 58 us -> 54.8 us
    pallas_call x1, Pallas kernels: 58 us -> 54.8 us  [step(): pl.pallas_call(kernel, out_shape=(jax.ShapeDtypeStruct((LAB, D), F32), ja...]
where the time goes in v4:
time: 61.7 us; the launch traced here: 61.2 us
  Pallas kernels  54.8 us (89%)
  local copies, waits for them, and re-layouts  3.02 us (5%)
  other arithmetic  2.77 us (4%)
  between operations  0.66 us (1%)
    pallas_call x1, Pallas kernels, step(): pl.pallas_call(kernel, out_shape=(jax.ShapeDtypeStruct((LAB, D), F32), ja...  54.8 us
    unnamed x8, local copies, waits for them, and re-layouts  3.02 us
    sub x1, other arithmetic, body(): new_weights = weights - step_rate * new_momentum  2 us

profile of v4, /device:TPU:1, one launch (start us, length us, event | category | flops | bytes accessed | tf_op | source)
XLA Modules:
  0.0 61.2 jit_solution(17857578220357464444)
XLA Ops:
  0.6 0.0 copy-start
  0.6 1.4 %copy-done = f32[512,768]{1,0:T(8,128)S(1)} copy-done((f32[512,768]{1,0:T(8,128)S(1)}, f32[512,768]{1,0:T(8,128)}, u32[]{:S(2)}) %copy-start) | copy-done | bytes 1572888
  2.0 0.0 copy-start.1
  2.0 0.9 %copy-done.1 = bf16[128,768]{1,0:T(8,128)(2,1)S(1)} copy-done((bf16[128,768]{1,0:T(8,128)(2,1)S(1)}, bf16[128,768]{1,0:T(8,128)(2,1)}, u32[]{:S(2)}) %copy-start.1) | copy-done | bytes 196632
  3.0 0.0 copy-start.2
  3.0 0.7 %copy-done.2 = s32[128,8]{0,1:T(8,128)S(1)} copy-done((s32[128,8]{0,1:T(8,128)S(1)}, s32[128,8]{0,1:T(8,128)}, u32[]{:S(2)}) %copy-start.2) | copy-done | bytes 4120
  3.7 0.0 copy-start.3
  3.7 54.8 %step.1 = (f32[512,768]{1,0:T(8,128)S(1)}, bf16[128,768]{1,0:T(8,128)(2,1)S(1)}) custom-call(bf16[128,768]{1,0:T(8,128)(2,1)S(1)} %copy-done.1, s32[8,128]{1,0:T(8,128)S(1)} %bitcast.1, f32[512,768]{1,0:T(8,128)S(1)} %copy-done), custom_call_target="tpu_custom_call" | custom-call | tf_op jit(solution)/shard_map/step/pallas_call | solution.py:386
  58.4 0.0 copy-done.3
  58.4 2.0 %multiply_subtract_fusion = (f32[512,768]{1,0:T(8,128)}, f32[512,768]{1,0:T(8,128)}) fusion(f32[512,768]{1,0:T(8,128)S(1)} %copy-done, f32[512,768]{1,0:T(8,128)S(1)} %get-tuple-element.5, f32[512,768]{1,0:T(8,128)S(1)} %copy-done.3), kind=kLoop, calls=%fused_computation | loop fusion | flops 1572864 | bytes 7864320 | tf_op jit(solution)/shard_map/sub | solution.py:427
  60.4 0.8 %convert_element_type.3 = f32[128,768]{1,0:T(8,128)} convert(bf16[128,768]{1,0:T(8,128)(2,1)S(1)} %get-tuple-element.6) | non-fusion elementwise | flops 98304 | bytes 589824 | tf_op jit(solution)/shard_map/convert_element_type | solution.py:428
Async XLA Ops:
  0.6 1.4 %copy-start = (f32[512,768]{1,0:T(8,128)S(1)}, f32[512,768]{1,0:T(8,128)}, u32[]{:S(2)}) copy-start(f32[512,768]{1,0:T(8,128)} %w_in.1) | copy-start | bytes 4718596
  2.0 0.9 %copy-start.1 = (bf16[128,768]{1,0:T(8,128)(2,1)S(1)}, bf16[128,768]{1,0:T(8,128)(2,1)}, u32[]{:S(2)}) copy-start(bf16[128,768]{1,0:T(8,128)(2,1)} %q_in.1) | copy-start | bytes 589828
  3.0 0.7 %copy-start.2 = (s32[128,8]{0,1:T(8,128)S(1)}, s32[128,8]{0,1:T(8,128)}, u32[]{:S(2)}) copy-start(s32[128,8]{0,1:T(8,128)} %param.5) | copy-start | bytes 12292
  3.7 54.8 %copy-start.3 = (f32[512,768]{1,0:T(8,128)S(1)}, f32[512,768]{1,0:T(8,128)}, u32[]{:S(2)}) copy-start(f32[512,768]{1,0:T(8,128)} %param.7) | copy-start | bytes 4718596

commit v5 on v4

--- a/solution.py
+++ b/solution.py
@@ -340,13 +340,13 @@
             start(("gc", way, i), GCS.at[n, i], GCR.at[n, i], partner)
     reduce_z(2)
     reduce_z(6)
-    reduce_last(4)
-    reduce_last(0)
     for i in range(SUB):
         for n, (way, base) in enumerate((("+", 2 * LAB), ("-", 3 * LAB))):
             arrived(("gc", way, i))
             GXS[n, i] = (WG[base + i * PIECE:base + (i + 1) * PIECE] + GCR[n, i].astype(F32)).astype(BF16)
             start(("gx", way, i), GXS.at[n, i], GXR.at[n, i], x_of["-" if way == "+" else "+"])
+    reduce_last(4)
+    reduce_last(0)
     for i in range(2):
         GOS[i] = WG[LAB + i * half:LAB + (i + 1) * half].astype(BF16)
         start(("go", i), GOS.at[i], GOR.at[i], partner)

time: 61.7 us -> 67.1 us (1.088)
  Pallas kernels: 54.8 us -> 60.5 us
    pallas_call x1, Pallas kernels: 54.8 us -> 60.5 us  [step(): pl.pallas_call(kernel, out_shape=(jax.ShapeDtypeStruct((LAB, D), F32), ja...]
where the time goes in v5:
time: 67.1 us; the launch traced here: 67 us
  Pallas kernels  60.5 us (90%)
  local copies, waits for them, and re-layouts  3.02 us (5%)
  other arithmetic  2.77 us (4%)
    pallas_call x1, Pallas kernels, step(): pl.pallas_call(kernel, out_shape=(jax.ShapeDtypeStruct((LAB, D), F32), ja...  60.5 us
    unnamed x8, local copies, waits for them, and re-layouts  3.02 us
    sub x1, other arithmetic, body(): new_weights = weights - step_rate * new_momentum  2 us

profile of v5, /device:TPU:1, one launch (start us, length us, event | category | flops | bytes accessed | tf_op | source)
XLA Modules:
  0.0 67.0 jit_solution(8077689027338073269)
XLA Ops:
  0.6 0.0 copy-start
  0.6 1.4 %copy-done = f32[512,768]{1,0:T(8,128)S(1)} copy-done((f32[512,768]{1,0:T(8,128)S(1)}, f32[512,768]{1,0:T(8,128)}, u32[]{:S(2)}) %copy-start) | copy-done | bytes 1572888
  2.0 0.0 copy-start.1
  2.0 0.9 %copy-done.1 = bf16[128,768]{1,0:T(8,128)(2,1)S(1)} copy-done((bf16[128,768]{1,0:T(8,128)(2,1)S(1)}, bf16[128,768]{1,0:T(8,128)(2,1)}, u32[]{:S(2)}) %copy-start.1) | copy-done | bytes 196632
  3.0 0.0 copy-start.2
  3.0 0.7 %copy-done.2 = s32[128,8]{0,1:T(8,128)S(1)} copy-done((s32[128,8]{0,1:T(8,128)S(1)}, s32[128,8]{0,1:T(8,128)}, u32[]{:S(2)}) %copy-start.2) | copy-done | bytes 4120
  3.7 0.0 copy-start.3
  3.7 60.5 %step.1 = (f32[512,768]{1,0:T(8,128)S(1)}, bf16[128,768]{1,0:T(8,128)(2,1)S(1)}) custom-call(bf16[128,768]{1,0:T(8,128)(2,1)S(1)} %copy-done.1, s32[8,128]{1,0:T(8,128)S(1)} %bitcast.1, f32[512,768]{1,0:T(8,128)S(1)} %copy-done), custom_call_target="tpu_custom_call" | custom-call | tf_op jit(solution)/shard_map/step/pallas_call | solution.py:386
  64.2 0.0 copy-done.3
  64.2 2.0 %multiply_subtract_fusion = (f32[512,768]{1,0:T(8,128)}, f32[512,768]{1,0:T(8,128)}) fusion(f32[512,768]{1,0:T(8,128)S(1)} %copy-done, f32[512,768]{1,0:T(8,128)S(1)} %get-tuple-element.5, f32[512,768]{1,0:T(8,128)S(1)} %copy-done.3), kind=kLoop, calls=%fused_computation | loop fusion | flops 1572864 | bytes 7864320 | tf_op jit(solution)/shard_map/sub | solution.py:427
  66.2 0.8 %convert_element_type.3 = f32[128,768]{1,0:T(8,128)} convert(bf16[128,768]{1,0:T(8,128)(2,1)S(1)} %get-tuple-element.6) | non-fusion elementwise | flops 98304 | bytes 589824 | tf_op jit(solution)/shard_map/convert_element_type | solution.py:428
Async XLA Ops:
  0.6 1.4 %copy-start = (f32[512,768]{1,0:T(8,128)S(1)}, f32[512,768]{1,0:T(8,128)}, u32[]{:S(2)}) copy-start(f32[512,768]{1,0:T(8,128)} %w_in.1) | copy-start | bytes 4718596
  2.0 0.9 %copy-start.1 = (bf16[128,768]{1,0:T(8,128)(2,1)S(1)}, bf16[128,768]{1,0:T(8,128)(2,1)}, u32[]{:S(2)}) copy-start(bf16[128,768]{1,0:T(8,128)(2,1)} %q_in.1) | copy-start | bytes 589828
  3.0 0.7 %copy-start.2 = (s32[128,8]{0,1:T(8,128)S(1)}, s32[128,8]{0,1:T(8,128)}, u32[]{:S(2)}) copy-start(s32[128,8]{0,1:T(8,128)} %param.5) | copy-start | bytes 12292
  3.7 60.5 %copy-start.3 = (f32[512,768]{1,0:T(8,128)S(1)}, f32[512,768]{1,0:T(8,128)}, u32[]{:S(2)}) copy-start(f32[512,768]{1,0:T(8,128)} %param.7) | copy-start | bytes 4718596
